TPU v7x, 1024 devices: a whole 4x4x32 slice. The times are simulated.
1024 devices in a mesh: blk: 64 (over z, core), rep: 16 (over x, y).
Axes of the slice: x: 4, y: 4, z: 32, core: 2. Of those that a mesh axis runs over, the one named last changes fastest.
Arguments:
- t_slab: bfloat16 [16, 1024, 64, 1024], P('rep', 'blk'), may hold values from -12 to 12
- w_cycle: bfloat16 [16, 1, 1024, 1024], P('rep'), may hold values from -0.75 to 0.75
- k_irrep: int32 [16], P('rep'), may hold values from 0 to 7
- i_irrep: int32 [64], replicated, may hold values from 0 to 7, as said below
- j_irrep: int32 [1], replicated, may hold values from 0 to 7
- tile_irrep: int32 [8], replicated, may hold values from 0 to 7, each once
- i_energy: float32 [64], replicated, may hold values from -2.5 to -0.5
- j_energy: float32 [1], replicated, may hold values from -2.5 to -0.5
- vir_energy: float32 [1024], replicated, may hold values from 0.3 to 3
Outputs:
- amplitude_update: float32 [1, 64, 1024, 1024], P(None, None, 'blk', 'rep')
Inputs may be any that keep to these rules, and one draw needn't show every extreme that they name: tile_irrep holds each of the 8 irreps exactly once. The orbitals i come in 8 runs of 8 consecutive orbitals; i_irrep is the same within a run, and each irrep labels exactly one run.
All inputs are finite; a program needn't handle non-finite values.
Results may differ from a plain program's by a relative error of at most 0.0003.
Values may be sent and summed in bfloat16 or wider, within the bound.
A program may use at most 32 MiB of HBM per device.

v0:
```python
import jax
import jax.numpy as jnp
from jax import lax
from jax.sharding import PartitionSpec as P

TILE = 128


def label_virtual(tile_irrep, count):
    tile_of = jnp.arange(count, dtype=jnp.int32) // TILE
    tiles = jnp.arange(tile_irrep.shape[0], dtype=jnp.int32)
    return jnp.sum(jnp.where(tile_of[:, None] == tiles[None, :], tile_irrep[None, :], 0), axis=1)


def masked(block, first_label, second_label, third_label, fourth_label):
    first = jnp.bitwise_xor(first_label[:, None, None, None], second_label[None, :, None, None])
    second = jnp.bitwise_xor(third_label[None, None, :, None], fourth_label[None, None, None, :])
    keep = jnp.bitwise_xor(first, second) == 0
    return jnp.where(keep, block, jnp.zeros((), block.dtype))


def shards(t_slab, w_cycle, k_irrep, i_irrep, j_irrep, tile_irrep, i_energy, j_energy, vir_energy):
    blk_count = lax.axis_size("blk")
    rep_count = lax.axis_size("rep")
    k_rows, c_width, rows_i, full_width = t_slab.shape
    rows_j = w_cycle.shape[1]
    vir_irrep = label_virtual(tile_irrep, full_width)
    a_width = full_width // blk_count
    b_width = full_width // rep_count
    a_start = lax.axis_index("blk") * a_width
    b_start = lax.axis_index("rep") * b_width
    c_label = lax.dynamic_slice_in_dim(vir_irrep, lax.axis_index("blk") * c_width, c_width, 0)
    held = masked(t_slab, k_irrep, c_label, i_irrep, vir_irrep)
    outgoing = held.reshape(k_rows, c_width, rows_i, blk_count, a_width).transpose(3, 0, 1, 2, 4)
    outgoing = outgoing.reshape(blk_count, k_rows * c_width, rows_i * a_width)
    arrived = lax.all_to_all(outgoing, "blk", split_axis=0, concat_axis=0, tiled=True)
    left_side = arrived.reshape(blk_count, k_rows, c_width, rows_i * a_width).transpose(1, 0, 2, 3)
    left_side = left_side.reshape(k_rows, full_width, rows_i * a_width)
    right_side = masked(w_cycle, k_irrep, j_irrep, vir_irrep, vir_irrep)
    right_side = right_side.transpose(0, 2, 1, 3).reshape(k_rows, full_width, rows_j * full_width)
    partial_value = lax.dot_general(
        left_side, right_side, (((0, 1), (0, 1)), ((), ())), preferred_element_type=jnp.float32
    )
    arranged = partial_value.reshape(rows_i * a_width, rows_j, rep_count, b_width).transpose(
        0, 2, 1, 3
    )
    arranged = arranged.reshape(rows_i * a_width, rep_count * rows_j * b_width)
    summed = lax.psum_scatter(arranged, "rep", scatter_dimension=1, tiled=True)
    result = summed.reshape(rows_i, a_width, rows_j, b_width)
    result = result.transpose(2, 0, 1, 3)
    b_energy = lax.dynamic_slice_in_dim(vir_energy, b_start, b_width, 0)
    a_energy = lax.dynamic_slice_in_dim(vir_energy, a_start, a_width, 0)
    denom = (
        a_energy[None, None, :, None]
        + b_energy[None, None, None, :]
        - i_energy[None, :, None, None]
        - j_energy[:, None, None, None]
    )
    return result / denom


def solution(mesh):
    in_specs = (
        P("rep", "blk", None, None),
        P("rep", None, None, None),
        P("rep"),
        P(),
        P(),
        P(),
        P(),
        P(),
        P(),
    )
    out_specs = P(None, None, "blk", "rep")
    return jax.shard_map(shards, mesh=mesh, in_specs=in_specs, out_specs=out_specs, check_vma=False)
```

profile of v0, /device:TPU:1, one launch (start us, length us, event | category | flops | bytes accessed | tf_op | source)
XLA Modules:
  0.0 371.6 jit_solution(15546219842093500108)
XLA Ops:
  6.5 0.0 copy-start.2
  6.5 0.0 copy-start.1
  6.5 4.8 %copy.22 = bf16[1,16,64,1024]{2,3,1,0:T(8,128)(2,1)} copy(bf16[1,16,64,1024]{3,2,1,0:T(8,128)(2,1)} %param.9) | data formatting | bytes 4194304 | tf_op args[0]
  12.0 0.0 copy-done.2
  12.0 0.1 select_reduce_fusion
  12.1 0.0 copy-done.1
  12.1 0.2 broadcast_xor_fusion
  12.3 0.1 dynamic-slice_xor_fusion
  12.4 5.6 %fusion = bf16[1,16,64,1024]{2,3,1,0:T(8,128)(2,1)} fusion(bf16[1,16,64,1024]{2,3,1,0:T(8,128)(2,1)} %copy.22, s32[64,1024]{0,1:T(8,128)S(1)} %broadcast_xor_fusion, s32[16]{0:T(128)S(1)} %dynamic-slice_xor_fusion), kind=kLoop, calls=%fused_computation.1 | loop fusion | flops 3145728 | bytes 4456512 | tf_op jit(solution)/shard_map/jit(_where)/select_n | solution.py:19
  18.0 8.9 %copy.23 = bf16[64,1,16,64,16]{0,4,3,2,1:T(8,128)(2,1)} copy(bf16[64,1,16,64,16]{3,4,0,2,1:T(8,128)(2,1)} %bitcast.15) | data formatting | bytes 4194304 | tf_op jit(solution)/shard_map/transpose | solution.py:34
  26.9 5.7 %copy.24 = bf16[64,16,1024]{2,1,0:T(8,128)(2,1)} copy(bf16[64,16,1024]{0,2,1:T(8,128)(2,1)} %bitcast.16) | data formatting | bytes 4194304 | tf_op jit(solution)/shard_map/reshape | solution.py:35
  32.6 30.4 %all-to-all-start = ((bf16[64,16,1024]{2,1,0:T(8,128)(2,1)}), bf16[64,16,1024]{2,1,0:T(8,128)(2,1)S(1)}, u32[]{:S(2)}, u32[]{:S(2)}) async-start(bf16[64,16,1024]{2,1,0:T(8,128)(2,1)} %copy.24), calls=%async_computation | async-start | bytes 4194304 | tf_op jit(solution)/shard_map/all_to_all | solution.py:36
  63.1 0.0 reduce-scatter.2.cloned.1.call-start
  63.8 197.0 %all-to-all-done = bf16[64,16,1024]{2,1,0:T(8,128)(2,1)S(1)} async-done(((bf16[64,16,1024]{2,1,0:T(8,128)(2,1)}), bf16[64,16,1024]{2,1,0:T(8,128)(2,1)S(1)}, u32[]{:S(2)}, u32[]{:S(2)}) %all-to-all-start) | async-done | bytes 2097184 | tf_op jit(solution)/shard_map/all_to_all | solution.py:36
  260.8 6.0 %fusion.3 = f32[1024,1024]{0,1:T(8,128)} fusion(bf16[1024,1024]{1,0:T(8,128)(2,1)S(1)} %bitcast.18, bf16[1,1,1024,1024]{3,2,1,0:T(8,128)(2,1)} %param.10, s32[1024]{0:T(1024)S(1)} %select_reduce_fusion, s32[]{:T(128)} %bitcast.5), kind=kOutput, calls=%fused_computation.5 | convolution fusion | flops 2151677952 | bytes 8392708 | tf_op jit(solution)/shard_map/dot_general | solution.py:41
  266.8 0.0 copy-start
  266.8 0.0 reduce-scatter.2.cloned.1.call-update
  267.5 0.8 dynamic_slice.10
  268.3 0.8 dynamic_slice.11
  269.0 0.1 broadcast_add_fusion
  269.1 93.6 %reduce-scatter.2.cloned.1.call-done = f32[1024,64]{0,1:T(8,128)} async-done(((f32[1024,1024]{0,1:T(8,128)}), f32[1024,64]{0,1:T(8,128)}) %reduce-scatter.2.cloned.1.call-update) | async-done | bytes 262160 | tf_op jit(solution)/shard_map/reduce_scatter | solution.py:48
  362.7 1.1 copy.25
  363.8 0.0 copy-done
  363.8 0.9 subtract_divide_fusion
  (1 shorter events, 0.0 us)
Async XLA Ops:
  6.5 5.5 %copy-start.2 = (s32[8]{0:T(128)S(1)}, s32[8]{0:T(128)}, u32[]{:S(2)}) copy-start(s32[8]{0:T(128)} %param.14) | copy-start | bytes 100
  6.5 5.6 %copy-start.1 = (s32[64]{0:T(128)S(1)}, s32[64]{0:T(128)}, u32[]{:S(2)}) copy-start(s32[64]{0:T(128)} %param.12) | copy-start | bytes 772
  32.6 228.1 %all-to-all-start = ((bf16[64,16,1024]{2,1,0:T(8,128)(2,1)}), bf16[64,16,1024]{2,1,0:T(8,128)(2,1)S(1)}, u32[]{:S(2)}, u32[]{:S(2)}) async-start(bf16[64,16,1024]{2,1,0:T(8,128)(2,1)} %copy.24), calls=%async_computation | async-start | bytes 4194304 | tf_op jit(solution)/shard_map/all_to_all | solution.py:36
  63.1 299.6 %reduce-scatter.2.cloned.1.call-start = ((), (), s32[]{:S(2)}) async-start(), calls=%async_computation.2 | async-start | bytes 4456448 | tf_op jit(solution)/shard_map/reduce_scatter | solution.py:48
  266.8 97.0 %copy-start = (f32[64]{0:T(128)S(1)}, f32[64]{0:T(128)}, u32[]{:S(2)}) copy-start(f32[64]{0:T(128)} %param.15) | copy-start | bytes 772
Sparse Core Ops, SparseCore 0:
  267.0 95.6 reduce-scatter.1
where the time goes:
time: 373 us; the launch traced here: 372 us
  waiting for transfers between devices  291 us (78%)
  starting transfers between devices  30.4 us (8%)
  local copies, waits for them, and re-layouts  22.1 us (6%)
  between operations  15.4 us (4%)
  other arithmetic  7.02 us (2%)
  matrix products  6.05 us (2%)
    all_to_all x1, waiting for transfers between devices, shards(): lax.all_to_all(outgoing, 'blk', split_axis=0, concat_axis=0, tiled=True)  197 us
    reduce_scatter x1, waiting for transfers between devices, shards(): summed = lax.psum_scatter(arranged, 'rep', scatter_dimension=1, tiled=True)  93.6 us
    all_to_all x1, starting transfers between devices, shards(): lax.all_to_all(outgoing, 'blk', split_axis=0, concat_axis=0, tiled=True)  30.4 us
    transpose x1, local copies, waits for them, and re-layouts, shards(): held.reshape(k_rows, c_width, rows_i, blk_count, a_width)  8.9 us
  transfers between devices with their start and end apart: 2, of which 2 were waited for; matrix products, arithmetic and copies ran while one was open for 0% of the time, Pallas kernels for 0%

commit v1 on v0

v1 whole, which is shorter than its diff:
```python
import functools

import jax
import jax.numpy as jnp
from jax import lax
from jax.experimental import pallas as pl
from jax.experimental.pallas import tpu as pltpu
from jax.sharding import PartitionSpec as P

TILE = 128
RUNS = 8
MESH = pl.DeviceIdType.MESH


def pick(position, scalars):
    label = jnp.zeros(position.shape, jnp.int32)
    for place, scalar in enumerate(scalars):
        label = jnp.where(position == place, scalar, label)
    return label


def swap_blocks(rows, width):
    count = len(rows)
    block = lax.broadcasted_iota(jnp.int32, rows[0].shape, 1) // width
    step = count // 2
    while step:
        low = (block // step) % 2 == 0
        new = list(rows)
        for i in range(count):
            if i & step == 0:
                j = i | step
                new[i] = jnp.where(low, rows[i], pltpu.roll(rows[j], step * width, 1))
                new[j] = jnp.where(low, pltpu.roll(rows[i], TILE - step * width, 1), rows[j])
        rows = new
        step //= 2
    return rows


def kernel(
    blk_count,
    rep_count,
    k_ref,
    i_ref,
    j_ref,
    tile_ref,
    t_hbm,
    w_hbm,
    out_ref,
    t_vm,
    w_vm,
    x_vm,
    wt_vm,
    send,
    recv,
    part_send,
    part_recv,
    local_sem,
    send_sem,
    recv_sem,
    part_send_sem,
    part_recv_sem,
):
    c_width, rows_i, full = t_vm.shape
    tiles = full // TILE
    run_len = rows_i // RUNS
    group = blk_count // tiles
    a_width = full // blk_count
    b_width = full // rep_count
    chips = blk_count // 2
    me_p = lax.axis_index("blk")
    me_r = lax.axis_index("rep")

    t_copy = pltpu.make_async_copy(t_hbm, t_vm, local_sem.at[0])
    t_copy.start()
    w_copy = pltpu.make_async_copy(w_hbm, w_vm, local_sem.at[1])
    w_copy.start()

    barrier = pltpu.get_barrier_semaphore()

    def greet_blk(step, carry):
        other = lax.rem(me_p + step, blk_count)
        pl.semaphore_signal(barrier, inc=1, device_id={"blk": other}, device_id_type=MESH)
        return carry

    def greet_rep(step, carry):
        other = lax.rem(me_r + step, rep_count)
        pl.semaphore_signal(barrier, inc=1, device_id={"rep": other}, device_id_type=MESH)
        return carry

    lax.fori_loop(1, blk_count, greet_blk, 0)
    lax.fori_loop(1, rep_count, greet_rep, 0)

    irreps = [tile_ref[t] for t in range(tiles)]
    c_irrep = tile_ref[me_p // group]
    row = lax.broadcasted_iota(jnp.int32, (rows_i, full), 0)
    col = lax.broadcasted_iota(jnp.int32, (rows_i, full), 1)
    run_label = pick(row // run_len, [i_ref[g * run_len] for g in range(RUNS)])
    a_label = pick(col // TILE, irreps)
    keep = (run_label ^ a_label) == (k_ref[0] ^ c_irrep)
    mask = jnp.where(keep, 1.0, 0.0).astype(jnp.bfloat16)
    row = lax.broadcasted_iota(jnp.int32, (run_len * c_width, 16 * c_width), 0)
    col = lax.broadcasted_iota(jnp.int32, (run_len * c_width, 16 * c_width), 1)
    chosen = (row % c_width == col // 16) & (row // c_width == col % run_len)
    order = jnp.where(chosen, 1.0, 0.0).astype(jnp.bfloat16)

    t_copy.wait()
    kept = []
    for c in range(c_width):
        held = t_vm[c] * mask
        kept.append(sum(held[16 * q : 16 * q + 16] for q in range(rows_i // 16)))
    kept = jnp.concatenate(kept, axis=0)
    x_vm[...] = jnp.dot(order, kept, preferred_element_type=jnp.float32)
    for t in range(tiles):
        blocks = [
            x_vm[i * c_width : (i + 1) * c_width, t * TILE : (t + 1) * TILE] for i in range(run_len)
        ]
        for u, block in enumerate(swap_blocks(blocks, a_width)):
            send[t * group + u] = block.astype(jnp.bfloat16)

    pl.semaphore_wait(barrier, blk_count - 1 + rep_count - 1)

    def send_blk(step, carry):
        ring = step // 2
        far = chips // 2 - (ring + 1) // 2
        shift = jnp.where(ring % 2 == 1, far, chips - far)
        other = lax.rem(me_p // 2 + shift, chips) * 2 + lax.rem(me_p + 1 + step, 2)
        pltpu.make_async_remote_copy(
            src_ref=send.at[other],
            dst_ref=recv.at[me_p],
            send_sem=send_sem,
            recv_sem=recv_sem,
            device_id={"blk": other},
            device_id_type=MESH,
        ).start()
        return carry

    lax.fori_loop(0, blk_count - 1, send_blk, 0)
    recv[me_p] = send[me_p]

    w_copy.wait()
    wanted = k_ref[0] ^ j_ref[0]

    def turn(t, carry):
        rows = pl.ds(pl.multiple_of(t * TILE, TILE), TILE)
        for b in range(tiles):
            tile = w_vm[rows, b * TILE : (b + 1) * TILE].astype(jnp.float32)
            tile = jnp.where(tile_ref[t] ^ irreps[b] == wanted, tile, 0.0)
            wt_vm[b * TILE : (b + 1) * TILE, rows] = tile.T.astype(jnp.bfloat16)
        return carry

    lax.fori_loop(0, tiles, turn, 0)

    others = pl.ds(0, blk_count - 1)
    pltpu.make_async_copy(send.at[others], recv.at[others], recv_sem).wait()
    left = recv[...].reshape(full, TILE)
    part = jnp.dot(wt_vm[...], left, preferred_element_type=jnp.float32)
    part_send[...] = part.reshape(rep_count, b_width, TILE)

    def send_rep(step, carry):
        other = lax.rem(me_r + step, rep_count)
        pltpu.make_async_remote_copy(
            src_ref=part_send.at[other],
            dst_ref=part_recv.at[me_r],
            send_sem=part_send_sem,
            recv_sem=part_recv_sem,
            device_id={"rep": other},
            device_id_type=MESH,
        ).start()
        return carry

    lax.fori_loop(1, rep_count, send_rep, 0)
    part_recv[me_r] = part_send[me_r]
    pltpu.make_async_copy(send.at[others], recv.at[others], send_sem).wait()
    others = pl.ds(0, rep_count - 1)
    pltpu.make_async_copy(part_send.at[others], part_recv.at[others], part_recv_sem).wait()
    total = part_recv[0]
    for r in range(1, rep_count):
        total = total + part_recv[r]
    out_ref[...] = total
    pltpu.make_async_copy(part_send.at[others], part_recv.at[others], part_send_sem).wait()


def shards(t_slab, w_cycle, k_irrep, i_irrep, j_irrep, tile_irrep, i_energy, j_energy, vir_energy):
    blk_count = lax.axis_size("blk")
    rep_count = lax.axis_size("rep")
    _, c_width, rows_i, full = t_slab.shape
    tiles = full // TILE
    run_len = rows_i // RUNS
    a_width = full // blk_count
    b_width = full // rep_count
    packed = run_len * a_width
    smem = pl.BlockSpec(memory_space=pltpu.SMEM)
    hbm = pl.BlockSpec(memory_space=pl.ANY)
    summed = pl.pallas_call(
        functools.partial(kernel, blk_count, rep_count),
        out_shape=jax.ShapeDtypeStruct((b_width, packed), jnp.float32),
        in_specs=[smem, smem, smem, smem, hbm, hbm],
        out_specs=pl.BlockSpec(memory_space=pltpu.VMEM),
        scratch_shapes=[
            pltpu.VMEM((c_width, rows_i, full), jnp.bfloat16),
            pltpu.VMEM((full, full), jnp.bfloat16),
            pltpu.VMEM((run_len * c_width, full), jnp.float32),
            pltpu.VMEM((full, full), jnp.bfloat16),
            pltpu.VMEM((blk_count, c_width, packed), jnp.bfloat16),
            pltpu.VMEM((blk_count, c_width, packed), jnp.bfloat16),
            pltpu.VMEM((rep_count, b_width, packed), jnp.float32),
            pltpu.VMEM((rep_count, b_width, packed), jnp.float32),
            pltpu.SemaphoreType.DMA((2,)),
            pltpu.SemaphoreType.DMA,
            pltpu.SemaphoreType.DMA,
            pltpu.SemaphoreType.DMA,
            pltpu.SemaphoreType.DMA,
        ],
        compiler_params=pltpu.CompilerParams(
            collective_id=0, has_side_effects=True, vmem_limit_bytes=32 * 2**20
        ),
    )(k_irrep, i_irrep, j_irrep, tile_irrep, t_slab[0], w_cycle[0, 0])

    p = lax.axis_index("blk")
    r = lax.axis_index("rep")
    a_energy = lax.dynamic_slice_in_dim(vir_energy, p * a_width, a_width, 0)
    b_energy = lax.dynamic_slice_in_dim(vir_energy, r * b_width, b_width, 0)
    a_irrep = tile_irrep[p * a_width // TILE]
    b_irrep = tile_irrep[r * b_width // TILE]
    value = summed.T.reshape(1, run_len, a_width, b_width)
    keep = i_irrep == (j_irrep[0] ^ a_irrep ^ b_irrep)
    denom = (
        a_energy[None, :, None]
        + b_energy[None, None, :]
        - i_energy[:, None, None]
        - j_energy[:, None, None]
    ).reshape(RUNS, run_len, a_width, b_width)
    keep = keep.reshape(RUNS, run_len, 1, 1)
    result = jnp.where(keep, value / denom, 0.0)
    return result.reshape(1, rows_i, a_width, b_width)


def solution(mesh):
    in_specs = (
        P("rep", "blk", None, None),
        P("rep", None, None, None),
        P("rep"),
        P(),
        P(),
        P(),
        P(),
        P(),
        P(),
    )
    out_specs = P(None, None, "blk", "rep")
    return jax.shard_map(shards, mesh=mesh, in_specs=in_specs, out_specs=out_specs, check_vma=False)
```

time: 373 us -> 78.4 us (0.21)
  waiting for transfers between devices: 291 us -> 0 us
  Pallas kernels: 0 us -> 65.4 us
  starting transfers between devices: 30.4 us -> 0 us
  local copies, waits for them, and re-layouts: 22.1 us -> 7.55 us
  between operations: 15.4 us -> 3.32 us
  matrix products: 6.05 us -> 0 us
  other arithmetic: 7.02 us -> 1.73 us
    all_to_all x1 -> x0, waiting for transfers between devices: 197 us -> none  [shards(): lax.all_to_all(outgoing, 'blk', split_axis=0, concat_axis=0, tiled=True)]
    reduce_scatter x1 -> x0, waiting for transfers between devices: 93.6 us -> none  [shards(): summed = lax.psum_scatter(arranged, 'rep', scatter_dimension=1, tiled=True)]
    pallas_call x0 -> x1, Pallas kernels: none -> 65.4 us  [shards(): pl.pallas_call(functools.partial(kernel, blk_count, rep_count), out_shape...]
    all_to_all x1 -> x0, starting transfers between devices: 30.4 us -> none  [shards(): lax.all_to_all(outgoing, 'blk', split_axis=0, concat_axis=0, tiled=True)]
    transpose x1, local copies, waits for them, and re-layouts: 8.9 us -> 0.09 us  [shards(): value = summed.T.reshape(1, run_len, a_width, b_width)]
    dot_general x1 -> x0, matrix products: 6.05 us -> none  [shards(): lax.dot_general(left_side, right_side, (((0, 1), (0, 1)), ((), ())), pref...]
    reshape x1 -> x0, local copies, waits for them, and re-layouts: 5.72 us -> none  [shards(): outgoing = outgoing.reshape(blk_count, k_rows * c_width, rows_i * a_width)]
    select_n x2 -> x1, other arithmetic: 5.65 us -> 1 us  [shards(): result = jnp.where(keep, value / denom, 0.0)]
  transfers between devices with their start and end apart: 2 -> 0, of which waited for: 2 -> 0; matrix products, arithmetic and copies ran while one was open for 0% -> 0% of each run, Pallas kernels for 0% -> 0%
where the time goes in v1:
time: 78.4 us; the launch traced here: 78 us
  Pallas kernels  65.4 us (83%)
  local copies, waits for them, and re-layouts  7.55 us (10%)
  between operations  3.32 us (4%)
  other arithmetic  1.73 us (2%)
    pallas_call x1, Pallas kernels, shards(): pl.pallas_call(functools.partial(kernel, blk_count, rep_count), out_shape...  65.4 us
    unnamed x10, local copies, waits for them, and re-layouts  4.5 us

profile of v1, /device:TPU:1, one launch (start us, length us, event | category | flops | bytes accessed | tf_op | source)
XLA Modules:
  0.0 78.0 jit_solution(13303697453603015330)
XLA Ops:
  1.9 0.8 dynamic_slice.15
  2.7 0.8 dynamic_slice.14
  3.5 1.4 %fusion.1 = (s32[1]{0:T(128)}, s32[1]{0:T(128)}) fusion(s32[8]{0:T(128)} %tile_ref.1, s32[]{:T(128)S(6)} %select_n.34, s32[]{:T(128)S(6)} %select_n.32), kind=kLoop, calls=%fused_computation.4 | loop fusion | bytes 24 | tf_op jit(solution)/shard_map/dynamic_slice | solution.py:224
  6.2 0.7 broadcast_compare_fusion
  6.9 0.1 broadcast_add_fusion
  6.9 0.0 copy-start
  6.9 1.6 %copy-done = bf16[1,16,64,1024]{3,2,1,0:T(8,128)(2,1)S(1)} copy-done((bf16[1,16,64,1024]{3,2,1,0:T(8,128)(2,1)S(1)}, bf16[1,16,64,1024]{3,2,1,0:T(8,128)(2,1)}, u32[]{:S(2)}) %copy-start) | copy-done | bytes 2097176
  8.5 0.0 copy-start.1
  8.5 1.6 %copy-done.1 = bf16[1,1,1024,1024]{3,2,1,0:T(8,128)(2,1)S(1)} copy-done((bf16[1,1,1024,1024]{3,2,1,0:T(8,128)(2,1)S(1)}, bf16[1,1,1024,1024]{3,2,1,0:T(8,128)(2,1)}, u32[]{:S(2)}) %copy-start.1) | copy-done | bytes 2097176
  10.1 0.0 copy-start.2
  10.1 0.7 copy-done.2
  10.8 0.0 copy-start.3
  10.8 0.7 copy-done.3
  11.4 0.0 copy-start.4
  11.4 65.4 %shard_map.91 = f32[64,128]{1,0:T(8,128)S(1)} custom-call(s32[1]{0:T(128)S(6)} %copy.12.k_ref, s32[64]{0:T(128)S(1)} %copy-done.3, s32[1]{0:T(128)S(6)} %copy.13.j_ref, s32[8]{0:T(128)S(1)} %copy-done.2, bf16[16,64,1024]{2,1,0:T(8,128)(2,1)S(1)} %bitcast.12, bf16[1024,1024]{1,0:T(8,128)(2,1)S(1)} %bitcast.13), custom_call_target="tpu_custom_call" | custom-call | tf_op jit(solution)/shard_map/pallas_call | solution.py:194
  76.9 0.1 copy.11
  77.0 0.0 copy-done.4
  77.0 1.0 %fusion = f32[1,64,16,64]{3,2,1,0:T(8,128)} fusion(f32[]{:T(128)} %bitcast.11, f32[64]{0:T(128)S(1)} %copy-done.4, f32[16,64]{1,0:T(8,128)S(1)} %broadcast_add_fusion, pred[64]{0:T(512)(128)(4,1)S(1)} %broadcast_compare_fusion, f32[1,64,16,64]{3,2,1,0:T(8,128)S(1)} %bitcast.15), kind=kLoop, calls=%fused_computation.1 | loop fusion | flops 262144 | bytes 528708 | tf_op jit(solution)/shard_map/jit(_where)/select_n | solution.py:234
  (1 shorter events, 0.0 us)
Async XLA Ops:
  6.9 1.6 %copy-start = (bf16[1,16,64,1024]{3,2,1,0:T(8,128)(2,1)S(1)}, bf16[1,16,64,1024]{3,2,1,0:T(8,128)(2,1)}, u32[]{:S(2)}) copy-start(bf16[1,16,64,1024]{3,2,1,0:T(8,128)(2,1)} %param.9) | copy-start | bytes 6291460
  8.5 1.6 %copy-start.1 = (bf16[1,1,1024,1024]{3,2,1,0:T(8,128)(2,1)S(1)}, bf16[1,1,1024,1024]{3,2,1,0:T(8,128)(2,1)}, u32[]{:S(2)}) copy-start(bf16[1,1,1024,1024]{3,2,1,0:T(8,128)(2,1)} %param.10) | copy-start | bytes 6291460
  10.1 0.7 copy-start.2
  10.8 0.7 copy-start.3
  11.4 65.6 %copy-start.4 = (f32[64]{0:T(128)S(1)}, f32[64]{0:T(128)}, u32[]{:S(2)}) copy-start(f32[64]{0:T(128)} %param.15) | copy-start | bytes 772

commit v2 on v1

v2 whole, which is shorter than its diff:
```python
import functools

import jax
import jax.numpy as jnp
from jax import lax
from jax.experimental import pallas as pl
from jax.experimental.pallas import tpu as pltpu
from jax.sharding import PartitionSpec as P

TILE = 128
RUNS = 8
FIRST_TILES = 2
AHEAD = 8
HALF = TILE // 2
MESH = pl.DeviceIdType.MESH


def pick(position, scalars):
    label = jnp.zeros(position.shape, jnp.int32)
    for place, scalar in enumerate(scalars):
        label = jnp.where(position == place, scalar, label)
    return label


def swap_blocks(rows, width):
    count = len(rows)
    block = lax.broadcasted_iota(jnp.int32, rows[0].shape, 1) // width
    step = count // 2
    while step:
        low = (block // step) % 2 == 0
        new = list(rows)
        for i in range(count):
            if i & step == 0:
                j = i | step
                new[i] = jnp.where(low, rows[i], pltpu.roll(rows[j], step * width, 1))
                new[j] = jnp.where(low, pltpu.roll(rows[i], TILE - step * width, 1), rows[j])
        rows = new
        step //= 2
    return rows


def kernel(
    blk_count,
    rep_count,
    k_hbm,
    i_hbm,
    j_hbm,
    tile_hbm,
    i_energy_hbm,
    j_energy_hbm,
    vir_hbm,
    t_hbm,
    w_hbm,
    out_ref,
    k_ref,
    i_ref,
    j_ref,
    tile_ref,
    i_energy,
    j_energy,
    vir_vm,
    t_vm,
    w_vm,
    wt_vm,
    denom_vm,
    left_vm,
    send,
    recv,
    part_send,
    part_recv,
    small_sem,
    t_sem,
    w_sem,
    ok_sem,
    here_sem,
    send_sem,
    recv_sem,
    part_send_sem,
    part_recv_sem,
):
    tiles, c_width, rows_i, _ = t_vm.shape
    full = tiles * TILE
    run_len = rows_i // RUNS
    group = blk_count // tiles
    a_width = full // blk_count
    b_width = full // rep_count
    chips = blk_count // 2
    first_tiles = FIRST_TILES
    first = first_tiles * group // 2
    me_p = lax.axis_index("blk")
    me_r = lax.axis_index("rep")
    chip = me_p // 2
    core = lax.rem(me_p, 2)
    sibling = me_p + 1 - 2 * core

    small = [
        pltpu.make_async_copy(source, target, small_sem.at[n])
        for n, (source, target) in enumerate(
            (
                (k_hbm, k_ref),
                (i_hbm, i_ref),
                (tile_hbm, tile_ref),
                (j_hbm, j_ref),
                (i_energy_hbm, i_energy),
                (j_energy_hbm, j_energy),
                (vir_hbm, vir_vm),
            )
        )
    ]
    for copy in small[:3]:
        copy.start()
    t_copies = [
        pltpu.make_async_copy(t_hbm.at[:, :, pl.ds(t * TILE, TILE)], t_vm.at[t], t_sem.at[t])
        for t in range(tiles)
    ]
    for copy in t_copies:
        copy.start()

    barrier = pltpu.get_barrier_semaphore()
    is_first = chip < first
    before = jnp.minimum(chip, first)

    def greet(**device):
        pl.semaphore_signal(barrier, inc=1, device_id=device, device_id_type=MESH)

    def greet_after(other, carry):
        greet(blk=other * 2)
        return carry

    def greet_last(other, carry):
        @pl.when(other != chip)
        def _():
            greet(blk=other * 2 + 1)

        return carry

    def greet_rep(step, carry):
        greet(blk=chip * 2 + 1, rep=lax.rem(me_r + step, rep_count))
        return carry

    greet(blk=sibling)

    @pl.when(is_first)
    def _():
        lax.fori_loop(chip + 1, chips, greet_after, 0)

    @pl.when(jnp.logical_not(is_first))
    def _():
        lax.fori_loop(first, chips, greet_last, 0)

    lax.fori_loop(1, rep_count, greet_rep, 0)

    w_copy = pltpu.make_async_copy(w_hbm, w_vm, w_sem)
    w_copy.start()
    for copy in small[3:]:
        copy.start()

    row = lax.broadcasted_iota(jnp.int32, (run_len * c_width, 16 * c_width), 0)
    col = lax.broadcasted_iota(jnp.int32, (run_len * c_width, 16 * c_width), 1)
    chosen = (row % c_width == col // 16) & (row // c_width == col % run_len)
    order = jnp.where(chosen, 1.0, 0.0).astype(jnp.bfloat16)
    for copy in small[:3]:
        copy.wait()
    irreps = [tile_ref[t] for t in range(tiles)]
    row = lax.broadcasted_iota(jnp.int32, (rows_i, TILE), 0)
    run_label = pick(row // run_len, [i_ref[g * run_len] for g in range(RUNS)])
    run_label = run_label ^ (k_ref[0] ^ tile_ref[me_p // group])

    low = lax.broadcasted_iota(jnp.int32, (8, TILE), 1) < HALF

    def pack(t, carry):
        lanes = pl.ds(pl.multiple_of(t * TILE, TILE), TILE)
        pltpu.make_async_copy(t_hbm.at[:, :, lanes], t_vm.at[t], t_sem.at[t]).wait()
        mask = jnp.where(run_label == tile_ref[t], 1.0, 0.0).astype(jnp.bfloat16)
        held = t_vm[t] * mask[None]
        held = sum(held[:, 16 * q : 16 * q + 16] for q in range(rows_i // 16))
        held = held.reshape(c_width * 16, TILE)
        held = jnp.dot(order, held, preferred_element_type=jnp.float32)
        blocks = [held[i * c_width : (i + 1) * c_width] for i in range(run_len)]
        for u, block in enumerate(swap_blocks(blocks, a_width)):
            above, below = block[:8], block[8:]
            one = jnp.where(low, above, pltpu.roll(below, HALF, 1))
            two = jnp.where(low, pltpu.roll(above, HALF, 1), below)
            send[0, t * group + u] = one.astype(jnp.bfloat16)
            send[1, t * group + u] = two.astype(jnp.bfloat16)
        return carry

    def send_to(half, other):
        pltpu.make_async_remote_copy(
            src_ref=send.at[half, other],
            dst_ref=recv.at[half, me_p],
            send_sem=send_sem.at[half],
            recv_sem=recv_sem.at[half],
            device_id={"blk": other},
            device_id_type=MESH,
        ).start()

    @pl.when(core == 0)
    def _():
        pl.semaphore_wait(barrier, 2 * before + 1)
        pl.semaphore_signal(ok_sem, inc=1, device_id={"blk": sibling}, device_id_type=MESH)

    @pl.when(core == 1)
    def _():
        pl.semaphore_wait(ok_sem, 1)

    def tell(other, carry):
        pl.semaphore_signal(
            here_sem.at[chip], inc=1, device_id={"blk": other * 2 + core}, device_id_type=MESH
        )
        return carry

    lax.fori_loop(0, before, tell, 0)
    lax.fori_loop(0, first_tiles, pack, 0)

    ahead = 2 * jnp.where(is_first, first, AHEAD)

    def send_before(step, carry):
        other = lax.rem(step, ahead)

        @pl.when((other // 2 < chip) | (other == sibling))
        def _():
            send_to(step // ahead, other)

        return carry

    lax.fori_loop(0, 2 * ahead, send_before, 0)

    lax.fori_loop(first_tiles, tiles, pack, 0)

    def send_chip(half, other):
        @pl.when(half == 0)
        def _():
            pl.semaphore_wait(here_sem.at[other], 1)

        send_to(half, other * 2 + core)
        send_to(half, other * 2 + 1 - core)

    def send_after(other, half):
        send_chip(half, other)
        return half

    def send_later(step, half):
        turn = step // 3
        place = lax.rem(step, 3)
        send_chip(half, jnp.where(place == 0, first + turn, chips - 2 * turn - place))
        return half

    @pl.when(is_first)
    def _():
        def send_half(half, carry):
            lax.fori_loop(chip + 1, first, send_after, half)
            lax.fori_loop(0, chips - first, send_later, half)
            return carry

        lax.fori_loop(0, 2, send_half, 0)

    @pl.when(core == 1)
    def _():
        greeted = 1 + 2 * (rep_count - 1)
        pl.semaphore_wait(
            barrier, jnp.where(is_first, greeted, greeted + 2 * (chips - first - 1))
        )
        pl.semaphore_signal(ok_sem, inc=1, device_id={"blk": sibling}, device_id_type=MESH)

    @pl.when(core == 0)
    def _():
        pl.semaphore_wait(ok_sem, 1)

    def send_last(step, half):
        ring = step // 2
        far = chips // 2 - (ring + 1) // 2
        shift = jnp.where(ring % 2 == 1, far, chips - far)
        other = lax.rem(chip + shift, chips) * 2 + lax.rem(me_p + 1 + step, 2)

        @pl.when(other >= 2 * AHEAD)
        def _():
            send_to(half, other)

        return half

    @pl.when(jnp.logical_not(is_first))
    def _():
        def send_half(half, carry):
            lax.fori_loop(0, blk_count - 1, send_last, half)
            return carry

        lax.fori_loop(0, 2, send_half, 0)

    for half in range(2):
        recv[half, me_p] = send[half, me_p]

    for copy in small[3:]:
        copy.wait()
    wanted = k_ref[0] ^ j_ref[0]
    w_copy.wait()

    def turn(t, carry):
        rows = pl.ds(pl.multiple_of(t * TILE, TILE), TILE)
        for b in range(tiles):
            tile = w_vm[rows, b * TILE : (b + 1) * TILE].astype(jnp.float32)
            tile = jnp.where(tile_ref[t] ^ irreps[b] == wanted, tile, 0.0)
            tile = tile.reshape(group, 2, 8, TILE)
            tile = jnp.concatenate([tile[:, n].reshape(HALF, TILE) for n in range(2)], axis=0)
            wt_vm[b * TILE : (b + 1) * TILE, rows] = tile.T.astype(jnp.bfloat16)
        return carry

    lax.fori_loop(0, tiles, turn, 0)

    a_start = me_p * a_width
    b_start = me_r * b_width
    run_wanted = j_ref[0] ^ tile_ref[a_start // TILE] ^ tile_ref[b_start // TILE]
    met = [i_ref[g * run_len] == run_wanted for g in range(RUNS)]
    row = lax.broadcasted_iota(jnp.int32, (a_width, TILE), 0)
    col = lax.broadcasted_iota(jnp.int32, (a_width, TILE), 1)
    a_row = vir_vm[pl.ds(a_start // TILE, 1), :]
    a_energy = jnp.sum(
        jnp.where(col == row + lax.rem(a_start, TILE), a_row, 0.0), axis=1, keepdims=True
    )
    b_row = vir_vm[pl.ds(b_start // TILE, 1), :]
    b_row = jnp.where(lax.rem(b_start, TILE) == 0, b_row, pltpu.roll(b_row, TILE - b_width, 1))
    for i in range(run_len):
        energy = i_energy[i]
        for g in range(1, RUNS):
            energy = jnp.where(met[g], i_energy[g * run_len + i], energy)
        rows = pl.ds(i * a_width, a_width)
        denom_vm[rows] = a_energy + b_row - energy - j_energy[0]

    others = pl.ds(0, blk_count - 1)
    wide_low = lax.broadcasted_iota(jnp.int32, (b_width // 2, TILE), 1) < HALF
    side = 4
    lines = side * b_width

    def send_rep(step, half):
        other = (lax.rem(me_r // side + step // side, side)) * side + lax.rem(me_r + step, side)

        @pl.when(other != me_r)
        def _():
            pltpu.make_async_remote_copy(
                src_ref=part_send.at[half, other],
                dst_ref=part_recv.at[half, me_r],
                send_sem=part_send_sem.at[half],
                recv_sem=part_recv_sem.at[half],
                device_id={"rep": other},
                device_id_type=MESH,
            ).start()

        return half

    for half in range(2):
        pltpu.make_async_copy(
            send.at[half, others], recv.at[half, others], recv_sem.at[half]
        ).wait()
        pieces = []
        for t in range(tiles):
            piece = recv[half, t * group : (t + 1) * group].astype(jnp.float32)
            piece = piece.reshape(HALF, TILE)
            pieces += [piece, pltpu.roll(piece, HALF, 1)]
        left_vm[...] = jnp.concatenate(pieces, axis=0).astype(jnp.bfloat16)

        def reduce(step, carry, half=half):
            block = lax.rem(me_r // side + step, side)
            rows = pl.ds(pl.multiple_of(block * lines, lines), lines)
            part = jnp.dot(wt_vm[rows, :], left_vm[...], preferred_element_type=jnp.float32)
            for n in range(side):
                above = part[n * b_width : n * b_width + b_width // 2]
                below = part[n * b_width + b_width // 2 : (n + 1) * b_width]
                part_send[half, block * side + n] = jnp.where(
                    wide_low, above, pltpu.roll(below, HALF, 1)
                )
            lax.fori_loop(step * side, (step + 1) * side, send_rep, half)
            return carry

        lax.fori_loop(0, side, reduce, 0)
        part_recv[half, me_r] = part_send[half, me_r]
    peers = pl.ds(0, rep_count - 1)
    totals = []
    for half in range(2):
        pltpu.make_async_copy(
            part_send.at[half, peers], part_recv.at[half, peers], part_recv_sem.at[half]
        ).wait()
        total = part_recv[half, 0]
        for r in range(1, rep_count):
            total = total + part_recv[half, r]
        totals.append(total)
    above = jnp.where(wide_low, totals[0], pltpu.roll(totals[1], HALF, 1))
    below = jnp.where(wide_low, pltpu.roll(totals[0], HALF, 1), totals[1])
    value = jnp.concatenate([above, below], axis=0).T / denom_vm[:, :b_width]
    for i in range(run_len):
        block = value[i * a_width : (i + 1) * a_width]
        for g in range(RUNS):
            out_ref[g * run_len + i] = jnp.where(met[g], block, 0.0)
    for half in range(2):
        pltpu.make_async_copy(
            send.at[half, others], recv.at[half, others], send_sem.at[half]
        ).wait()
        pltpu.make_async_copy(
            part_send.at[half, peers], part_recv.at[half, peers], part_send_sem.at[half]
        ).wait()


def shards(t_slab, w_cycle, k_irrep, i_irrep, j_irrep, tile_irrep, i_energy, j_energy, vir_energy):
    blk_count = lax.axis_size("blk")
    rep_count = lax.axis_size("rep")
    _, c_width, rows_i, full = t_slab.shape
    tiles = full // TILE
    run_len = rows_i // RUNS
    a_width = full // blk_count
    b_width = full // rep_count
    packed = run_len * a_width
    hbm = pl.BlockSpec(memory_space=pltpu.HBM)
    result = pl.pallas_call(
        functools.partial(kernel, blk_count, rep_count),
        out_shape=jax.ShapeDtypeStruct((rows_i, a_width, b_width), jnp.float32),
        in_specs=[hbm] * 9,
        out_specs=pl.BlockSpec(memory_space=pltpu.VMEM),
        scratch_shapes=[
            pltpu.SMEM((1,), jnp.int32),
            pltpu.SMEM((rows_i,), jnp.int32),
            pltpu.SMEM((1,), jnp.int32),
            pltpu.SMEM((tiles,), jnp.int32),
            pltpu.SMEM((rows_i,), jnp.float32),
            pltpu.SMEM((1,), jnp.float32),
            pltpu.VMEM((tiles, TILE), jnp.float32),
            pltpu.VMEM((tiles, c_width, rows_i, TILE), jnp.bfloat16),
            pltpu.VMEM((full, full), jnp.bfloat16),
            pltpu.VMEM((full, full), jnp.bfloat16),
            pltpu.VMEM((packed, TILE), jnp.float32),
            pltpu.VMEM((full, packed), jnp.bfloat16),
            pltpu.VMEM((2, blk_count, c_width // 2, packed), jnp.bfloat16),
            pltpu.VMEM((2, blk_count, c_width // 2, packed), jnp.bfloat16),
            pltpu.VMEM((2, rep_count, b_width // 2, packed), jnp.float32),
            pltpu.VMEM((2, rep_count, b_width // 2, packed), jnp.float32),
            pltpu.SemaphoreType.DMA((7,)),
            pltpu.SemaphoreType.DMA((tiles,)),
            pltpu.SemaphoreType.DMA,
            pltpu.SemaphoreType.REGULAR,
            pltpu.SemaphoreType.REGULAR((blk_count // 2,)),
            pltpu.SemaphoreType.DMA((2,)),
            pltpu.SemaphoreType.DMA((2,)),
            pltpu.SemaphoreType.DMA((2,)),
            pltpu.SemaphoreType.DMA((2,)),
        ],
        compiler_params=pltpu.CompilerParams(
            collective_id=0, has_side_effects=True, vmem_limit_bytes=62 * 2**20
        ),
    )(
        k_irrep,
        i_irrep,
        j_irrep,
        tile_irrep,
        i_energy,
        j_energy,
        vir_energy.reshape(tiles, TILE),
        t_slab[0],
        w_cycle[0, 0],
    )
    return result[None]


def solution(mesh):
    in_specs = (
        P("rep", "blk", None, None),
        P("rep", None, None, None),
        P("rep"),
        P(),
        P(),
        P(),
        P(),
        P(),
        P(),
    )
    out_specs = P(None, None, "blk", "rep")
    return jax.shard_map(shards, mesh=mesh, in_specs=in_specs, out_specs=out_specs, check_vma=False)
```

time: 78.4 us -> 57.6 us (0.73)
  the two profiles are of different devices: /device:TPU:1 before, /device:TPU:61 now
where the time goes in v2:
time: 57.6 us; the launch traced here: 57.4 us
  Pallas kernels  53.5 us (93%)
  between operations  1.95 us (3%)
  local copies, waits for them, and re-layouts  1.87 us (3%)
    pallas_call x1, Pallas kernels, shards(): pl.pallas_call(functools.partial(kernel, blk_count, rep_count), out_shape...  53.5 us
    unnamed x1, local copies, waits for them, and re-layouts  1.87 us

profile of v2, /device:TPU:61, one launch (start us, length us, event | category | flops | bytes accessed | tf_op | source)
XLA Modules:
  0.0 57.4 jit_solution(13081685034409561901)
XLA Ops:
  1.9 53.5 %shard_map.91 = f32[64,16,64]{2,1,0:T(8,128)} custom-call(s32[1]{0:T(128)S(6)} %copy.11.k_hbm, s32[64]{0:T(128)} %i_hbm.1, s32[1]{0:T(128)S(6)} %copy.12.j_hbm, s32[8]{0:T(128)} %tile_hbm.1, f32[64]{0:T(128)} %i_energy_hbm.1, f32[1]{0:T(128)S(6)} %copy.13.j_energy_hbm, f32[8,128]{1,0:T(8,128)} %bitcast.7, bf16[16,64,1024]{2,1,0:T(8,128)(2,1)} %bitcast.4, ...), custom_call_target="tpu_custom_call" | custom-call | tf_op jit(solution)/shard_map/pallas_call | solution.py:412
  55.5 1.9 %copy.14 = f32[1,64,16,64]{3,2,1,0:T(8,128)} copy(f32[1,64,16,64]{3,2,1,0:T(8,128)} %bitcast.6) | data formatting | bytes 524288

commit v3 on v2

--- a/solution.py
+++ b/solution.py
@@ -12,6 +12,7 @@
 FIRST_TILES = 2
 AHEAD = 8
 HALF = TILE // 2
+EVERY = 4
 MESH = pl.DeviceIdType.MESH
 
 
@@ -224,71 +225,10 @@
 
         return carry
 
-    lax.fori_loop(0, 2 * ahead, send_before, 0)
+    in_time = chip < chips // 2
+    lax.fori_loop(0, jnp.where(in_time, 2, 1) * ahead, send_before, 0)
 
     lax.fori_loop(first_tiles, tiles, pack, 0)
-
-    def send_chip(half, other):
-        @pl.when(half == 0)
-        def _():
-            pl.semaphore_wait(here_sem.at[other], 1)
-
-        send_to(half, other * 2 + core)
-        send_to(half, other * 2 + 1 - core)
-
-    def send_after(other, half):
-        send_chip(half, other)
-        return half
-
-    def send_later(step, half):
-        turn = step // 3
-        place = lax.rem(step, 3)
-        send_chip(half, jnp.where(place == 0, first + turn, chips - 2 * turn - place))
-        return half
-
-    @pl.when(is_first)
-    def _():
-        def send_half(half, carry):
-            lax.fori_loop(chip + 1, first, send_after, half)
-            lax.fori_loop(0, chips - first, send_later, half)
-            return carry
-
-        lax.fori_loop(0, 2, send_half, 0)
-
-    @pl.when(core == 1)
-    def _():
-        greeted = 1 + 2 * (rep_count - 1)
-        pl.semaphore_wait(
-            barrier, jnp.where(is_first, greeted, greeted + 2 * (chips - first - 1))
-        )
-        pl.semaphore_signal(ok_sem, inc=1, device_id={"blk": sibling}, device_id_type=MESH)
-
-    @pl.when(core == 0)
-    def _():
-        pl.semaphore_wait(ok_sem, 1)
-
-    def send_last(step, half):
-        ring = step // 2
-        far = chips // 2 - (ring + 1) // 2
-        shift = jnp.where(ring % 2 == 1, far, chips - far)
-        other = lax.rem(chip + shift, chips) * 2 + lax.rem(me_p + 1 + step, 2)
-
-        @pl.when(other >= 2 * AHEAD)
-        def _():
-            send_to(half, other)
-
-        return half
-
-    @pl.when(jnp.logical_not(is_first))
-    def _():
-        def send_half(half, carry):
-            lax.fori_loop(0, blk_count - 1, send_last, half)
-            return carry
-
-        lax.fori_loop(0, 2, send_half, 0)
-
-    for half in range(2):
-        recv[half, me_p] = send[half, me_p]
 
     for copy in small[3:]:
         copy.wait()
@@ -325,6 +265,75 @@
             energy = jnp.where(met[g], i_energy[g * run_len + i], energy)
         rows = pl.ds(i * a_width, a_width)
         denom_vm[rows] = a_energy + b_row - energy - j_energy[0]
+
+    def send_chip(half, other):
+        @pl.when(half == 0)
+        def _():
+            pl.semaphore_wait(here_sem.at[other], 1)
+
+        send_to(half, other * 2 + core)
+        send_to(half, other * 2 + 1 - core)
+
+    def send_after(other, half):
+        send_chip(half, other)
+        return half
+
+    def send_later(step, half):
+        turn = step // 3
+        place = lax.rem(step, 3)
+        send_chip(half, jnp.where(place == 0, first + turn, chips - 2 * turn - place))
+        return half
+
+    @pl.when(is_first)
+    def _():
+        def send_half(half, carry):
+            lax.fori_loop(chip + 1, first, send_after, half)
+            lax.fori_loop(0, chips - first, send_later, half)
+            return carry
+
+        lax.fori_loop(0, 2, send_half, 0)
+
+    @pl.when(core == 1)
+    def _():
+        greeted = 1 + 2 * (rep_count - 1)
+        pl.semaphore_wait(
+            barrier, jnp.where(is_first, greeted, greeted + 2 * (chips - first - 1))
+        )
+        pl.semaphore_signal(ok_sem, inc=1, device_id={"blk": sibling}, device_id_type=MESH)
+
+    @pl.when(core == 0)
+    def _():
+        pl.semaphore_wait(ok_sem, 1)
+
+    def send_last(step, half):
+        place = jnp.where(lax.rem(step, 2) == 0, step // 2, blk_count - 2 - step // 2)
+        ring = place // 2
+        far = chips // 2 - (ring + 1) // 2
+        shift = jnp.where(ring % 2 == 1, far, chips - far)
+        other = lax.rem(chip + shift, chips) * 2 + lax.rem(me_p + 1 + place, 2)
+
+        @pl.when((other >= 2 * AHEAD) & (step < blk_count - 1))
+        def _():
+            send_to(half, other)
+
+        turn = step // EVERY
+
+        @pl.when((half == 0) & (lax.rem(step, EVERY) == EVERY - 1) & (turn < 2 * AHEAD) & jnp.logical_not(in_time))
+        def _():
+            send_to(1, turn)
+
+        return half
+
+    @pl.when(jnp.logical_not(is_first))
+    def _():
+        def send_half(half, carry):
+            lax.fori_loop(0, blk_count, send_last, half)
+            return carry
+
+        lax.fori_loop(0, 2, send_half, 0)
+
+    for half in range(2):
+        recv[half, me_p] = send[half, me_p]
 
     others = pl.ds(0, blk_count - 1)
     wide_low = lax.broadcasted_iota(jnp.int32, (b_width // 2, TILE), 1) < HALF
@@ -409,6 +418,7 @@
     b_width = full // rep_count
     packed = run_len * a_width
     hbm = pl.BlockSpec(memory_space=pltpu.HBM)
+    held = functools.partial(pltpu.with_memory_space_constraint, memory_space=pltpu.HBM)
     result = pl.pallas_call(
         functools.partial(kernel, blk_count, rep_count),
         out_shape=jax.ShapeDtypeStruct((rows_i, a_width, b_width), jnp.float32),
@@ -442,18 +452,18 @@
             pltpu.SemaphoreType.DMA((2,)),
         ],
         compiler_params=pltpu.CompilerParams(
-            collective_id=0, has_side_effects=True, vmem_limit_bytes=62 * 2**20
+            collective_id=0, has_side_effects=True, vmem_limit_bytes=40 * 2**20
         ),
     )(
         k_irrep,
-        i_irrep,
+        held(i_irrep),
         j_irrep,
-        tile_irrep,
-        i_energy,
+        held(tile_irrep),
+        held(i_energy),
         j_energy,
-        vir_energy.reshape(tiles, TILE),
-        t_slab[0],
-        w_cycle[0, 0],
+        held(vir_energy.reshape(tiles, TILE)),
+        held(t_slab[0]),
+        held(w_cycle[0, 0]),
     )
     return result[None]
 

time: 57.6 us -> 54.9 us (0.953)
  the two profiles are of different devices: /device:TPU:61 before, /device:TPU:704 now
where the time goes in v3:
time: 54.9 us; the launch traced here: 54.7 us
  Pallas kernels  51.9 us (95%)
  between operations  1.95 us (4%)
  local copies, waits for them, and re-layouts  0.8 us (1%)
    pallas_call x1, Pallas kernels, shards(): pl.pallas_call(functools.partial(kernel, blk_count, rep_count), out_shape...  51.9 us

profile of v3, /device:TPU:704, one launch (start us, length us, event | category | flops | bytes accessed | tf_op | source)
XLA Modules:
  0.0 54.7 jit_solution(15038974650671299600)
XLA Ops:
  1.9 51.9 %shard_map.91 = f32[64,16,64]{2,1,0:T(8,128)S(1)} custom-call(s32[1]{0:T(128)S(6)} %copy.11.k_hbm, s32[64]{0:T(128)} %i_hbm.1, s32[1]{0:T(128)S(6)} %copy.12.j_hbm, s32[8]{0:T(128)} %tile_hbm.1, f32[64]{0:T(128)} %i_energy_hbm.1, f32[1]{0:T(128)S(6)} %copy.13.j_energy_hbm, f32[8,128]{1,0:T(8,128)} %bitcast.7, bf16[16,64,1024]{2,1,0:T(8,128)(2,1)} %bitcast.5, ...), custom_call_target="tpu_custom_call" | custom-call | tf_op jit(solution)/shard_map/pallas_call | solution.py:422
  53.9 0.8 %copy.14 = f32[1,64,16,64]{3,2,1,0:T(8,128)} copy(f32[1,64,16,64]{3,2,1,0:T(8,128)S(1)} %bitcast.4) | data formatting | bytes 524288

commit v4 on v3

--- a/solution.py
+++ b/solution.py
@@ -12,7 +12,7 @@
 FIRST_TILES = 2
 AHEAD = 8
 HALF = TILE // 2
-EVERY = 4
+EVERY = 1
 MESH = pl.DeviceIdType.MESH
 
 
@@ -340,8 +340,12 @@
     side = 4
     lines = side * b_width
 
+    def block_at(step):
+        ahead_by = jnp.where(step == 0, 2, jnp.where(step == 1, 1, jnp.where(step == 2, 3, 0)))
+        return lax.rem(me_r // side + ahead_by, side)
+
     def send_rep(step, half):
-        other = (lax.rem(me_r // side + step // side, side)) * side + lax.rem(me_r + step, side)
+        other = block_at(step // side) * side + lax.rem(me_r + step, side)
 
         @pl.when(other != me_r)
         def _():
@@ -368,7 +372,7 @@
         left_vm[...] = jnp.concatenate(pieces, axis=0).astype(jnp.bfloat16)
 
         def reduce(step, carry, half=half):
-            block = lax.rem(me_r // side + step, side)
+            block = block_at(step)
             rows = pl.ds(pl.multiple_of(block * lines, lines), lines)
             part = jnp.dot(wt_vm[rows, :], left_vm[...], preferred_element_type=jnp.float32)
             for n in range(side):

time: 54.9 us -> 54.7 us (level)
  the two profiles are of different devices: /device:TPU:704 before, /device:TPU:257 now
where the time goes in v4:
time: 54.7 us; the launch traced here: 54.5 us
  Pallas kernels  51.8 us (95%)
  between operations  1.95 us (4%)
  local copies, waits for them, and re-layouts  0.8 us (1%)
    pallas_call x1, Pallas kernels, shards(): pl.pallas_call(functools.partial(kernel, blk_count, rep_count), out_shape...  51.8 us

profile of v4, /device:TPU:257, one launch (start us, length us, event | category | flops | bytes accessed | tf_op | source)
XLA Modules:
  0.0 54.5 jit_solution(8591235432921408737)
XLA Ops:
  1.9 51.8 %shard_map.91 = f32[64,16,64]{2,1,0:T(8,128)S(1)} custom-call(s32[1]{0:T(128)S(6)} %copy.11.k_hbm, s32[64]{0:T(128)} %i_hbm.1, s32[1]{0:T(128)S(6)} %copy.12.j_hbm, s32[8]{0:T(128)} %tile_hbm.1, f32[64]{0:T(128)} %i_energy_hbm.1, f32[1]{0:T(128)S(6)} %copy.13.j_energy_hbm, f32[8,128]{1,0:T(8,128)} %bitcast.7, bf16[16,64,1024]{2,1,0:T(8,128)(2,1)} %bitcast.5, ...), custom_call_target="tpu_custom_call" | custom-call | tf_op jit(solution)/shard_map/pallas_call | solution.py:426
  53.7 0.8 %copy.14 = f32[1,64,16,64]{3,2,1,0:T(8,128)} copy(f32[1,64,16,64]{3,2,1,0:T(8,128)S(1)} %bitcast.4) | data formatting | bytes 524288
